TPU v7x, 32 devices: a whole 2x2x4 slice. The times are simulated.
32 devices in a mesh: stream: 2 (over x), batch: 16 (over z, y, core).
Axes of the slice: x: 2, y: 2, z: 4, core: 2. Of those that a mesh axis runs over, the one named last changes fastest.
Arguments:
- inputs: float32 [16, 2, 768, 768], P('batch', 'stream'), may hold values from -12 to 12
- text_pages: int32 [16, 768], P('batch'), may hold values from 0 to 3, as said below
- text_boxes: int32 [16, 2, 768], P('batch'), may hold values from 0 to 15
- norm_gains: float32 [2, 2, 768], P('stream'), may hold values from 0.1 to 1.9
- norm_shifts: float32 [2, 2, 768], P('stream'), may hold values from -1.8 to 1.8
- w_query: bfloat16 [2, 768, 768], P('stream'), may hold values from -0.21875 to 0.21875
- w_key: bfloat16 [2, 768, 768], P('stream'), may hold values from -0.21875 to 0.21875
- w_value: bfloat16 [2, 768, 768], P('stream'), may hold values from -0.21875 to 0.21875
- w_out: bfloat16 [2, 768, 768], P('stream'), may hold values from -1.75 to 1.75
- w_up: bfloat16 [2, 768, 3072], P('stream'), may hold values from -0.21875 to 0.21875
- up_bias: float32 [2, 3072], P('stream'), may hold values from -1.8 to 1.8
- w_down: bfloat16 [2, 3072, 768], P('stream'), may hold values from -0.109375 to 0.109375
- down_bias: float32 [2, 768], P('stream'), may hold values from -1.8 to 1.8
- box_table: float32 [2, 14, 12], P('stream'), may hold values from -4 to 4
- cotangent: float32 [16, 2, 768, 768], P('batch', 'stream'), may hold values from -6 to 6
Outputs:
- block_out: float32 [16, 2, 768, 768], P('batch', 'stream')
- grad_inputs: float32 [16, 2, 768, 768], P('batch', 'stream')
- grad_norm_gains: float32 [2, 2, 768], P('stream')
- grad_norm_shifts: float32 [2, 2, 768], P('stream')
- grad_w_query: float32 [2, 768, 768], P('stream', 'batch')
- grad_w_key: float32 [2, 768, 768], P('stream', 'batch')
- grad_w_value: float32 [2, 768, 768], P('stream', 'batch')
- grad_w_out: float32 [2, 768, 768], P('stream', 'batch')
- grad_w_up: float32 [2, 768, 3072], P('stream', 'batch')
- grad_up_bias: float32 [2, 3072], P('stream')
- grad_w_down: float32 [2, 3072, 768], P('stream', 'batch')
- grad_down_bias: float32 [2, 768], P('stream')
- grad_box_table: float32 [2, 14, 12], P('stream')
- stats: float32 [2], replicated
Inputs may be any that keep to these rules, and one draw needn't show every extreme that they name: `text_pages`: each row's text slots hold pages 0, 1, ..., 2 in order, each page non-empty, followed by padding slots marked 3; a row holds 384 to 768 text tokens, and both ends occur.
All inputs are finite; a program needn't handle non-finite values.
Results may differ from a plain program's by a relative error of at most 0.012.
Values may be sent and summed in bfloat16 or wider, within the bound.
A program may use at most 320 MiB of HBM per device.

v0:
```python
import jax
import jax.numpy as jnp
from jax import lax
from jax.experimental import pallas as pl
from jax.experimental.pallas import tpu as pltpu
from jax.sharding import PartitionSpec as P

GRID = 16
PAGES = 3
MESH = pl.DeviceIdType.MESH
LOG2E = 1.4426950408889634
LN2 = 0.6931471805599453
TOGETHER = 4
GELU_IN = 0.7978845608028654
GELU_CUBE = 0.044715
masked_fill = -1e30
f32 = jnp.float32
bf16 = jnp.bfloat16


def dot(left, right, form="nn"):
    dims = {"nn": (1, 0), "nt": (1, 1), "tn": (0, 0)}[form]
    return lax.dot_general(
        left, right, (((dims[0],), (dims[1],)), ((), ())), preferred_element_type=f32
    )


def stack(parts):
    return jnp.concatenate(parts, axis=0)


def plain_norm(values):
    center = values - jnp.mean(values, axis=-1, keepdims=True)
    inverse = lax.rsqrt(jnp.mean(center * center, axis=-1, keepdims=True) + 1e-05)
    return center * inverse, inverse


def norm_backward(grad_normed, plain, inverse, gain_row):
    scaled = grad_normed * gain_row
    first_mean = jnp.mean(scaled, axis=-1, keepdims=True)
    second_mean = jnp.mean(scaled * plain, axis=-1, keepdims=True)
    return inverse * (scaled - first_mean - plain * second_mean)


NAMES = (
    "ft", "wk", "wv", "back", "q_t", "k_t", "v_t", "att", "wo", "n2", "g2", "act", "gp",
    "wu", "wd", "sd", "sr",
)
RINGS = 4
SHARED = dict(
    nt=("n2",), wq=("act",), gm=("n2",), go=("g2",), dq=("wu", 0), dk=("wu", 1), dv=("wd", 0),
    send=("wd", 1), so=("sd", 0), sk=("sd", 1), sv=("sr", 0), sq=("sr", 1), sr1=("sr", 1),
    nt_again=("act",), wq_again=("gp",), sr0=("sr", 0),
)


def layer_kernel(
    x, cot, wq, wk, wv, wo, wup, wdn,
    up_bias, down_bias, gains, shifts, pages, boxes, rel_hbm,
    block_o, grad_o, nt_o, ga_o, down_o, up_o, wo_o, wq_o, hop_o, sums_o, late_o, table_o,
    buffers, wides, rel_table, bias, lse, delta, page_low, page_col, cells,
    cd, cr, yd, yr, zd, zr, hop, hop_in, sums_in, late_in, table_in, table_far,
    in_sem, w_sem, out_sem, csem, crem, ysem, yrem, zsem, zrem, xsem, xrem, hsem, hrem,
    asem, arem, bsem, brem, lsem, lrem, tsem, trem, gxs, gxr, gzs, gzr, gys, gyr, gcs, gcr,
):
    slots, width = x.shape
    heads = lse.shape[0]
    size = width // heads
    third = slots // 3
    thirds = [slice(part * third, (part + 1) * third) for part in range(3)]
    part_rows = width // 16
    st = lax.axis_index("stream")
    me = lax.axis_index("batch")
    c = lax.rem(me, 2)
    y = lax.rem(lax.div(me, 2), 2)
    z = lax.div(me, 4)
    place = lax.rem(me, 4)
    core_peer = (st, me + 1 - 2 * c)
    y_peer = (st, me + 2 - 4 * y)
    z_low = lax.rem(z, 2)
    z_high = lax.div(z, 2)
    one_peer = (st, me + 4 - 8 * z_low)
    two_peer = (st, me + 8 - 16 * z_high)
    z_at = [lax.rem(z + i, 4) for i in range(4)]
    z_peers = [(st, z_at[i] * 4 + place) for i in range(4)]
    place_at = [lax.rem(place + i, 4) for i in range(4)]
    place_peers = [(st, z * 4 + place_at[i]) for i in range(4)]
    x_peer = (1 - st, me)

    def span_of(j):
        return pl.ds(pl.multiple_of(j * third, third), third)

    def unrolled_third(step):
        for j in range(3):
            step(j, pl.ds(j * third, third))

    def each_third(step):
        def body(j, carry):
            step(j, span_of(j))
            return carry

        lax.fori_loop(0, 3, body, 0)

    S = dict(zip(NAMES, buffers))
    for name, (held, *at) in SHARED.items():
        S[name] = S[held].at[at[0]] if at else S[held]
    W = wides

    def slot(name):
        return S[name]

    def remote(source, target, send, recv, peer):
        return pltpu.make_async_remote_copy(
            source, target, send, recv, device_id=peer, device_id_type=MESH
        )

    singles = dict(
        x=(x, W[0]), cot=(cot, W[1]), wo=(wo, slot("wo")), wq=(wq, slot("wq")),
        x_again=(x, W[3]), wq_again=(wq, slot("wq_again")), nt_again=(nt_o, slot("nt_again")),
    )
    load_at = {name: i for i, name in enumerate(singles)}

    def load(name):
        return pltpu.make_async_copy(*singles[name], in_sem.at[load_at[name]])

    def chunk_of(t):
        return lax.rem(z + t + 1, 4)

    def up_load(t):
        at = pl.multiple_of(chunk_of(t) * width, width)
        two = lax.rem(t, 2)
        return pltpu.make_async_copy(
            wup.at[:, pl.ds(at, width)], S["wu"].at[two], w_sem.at[two, 0]
        )

    def down_load(t):
        at = pl.multiple_of(chunk_of(t) * width, width)
        two = lax.rem(t, 2)
        return pltpu.make_async_copy(
            wdn.at[pl.ds(at, width), :], S["wd"].at[two], w_sem.at[two, 1]
        )

    def act_load(t):
        return pltpu.make_async_copy(ga_o.at[t], W[1], w_sem.at[2, 0])

    def act_save(t):
        return pltpu.make_async_copy(W[2 + t % 2], ga_o.at[t], w_sem.at[2, 1 + t % 2])

    load("x").start()
    rel_copy = pltpu.make_async_copy(rel_hbm, rel_table, out_sem.at[1])
    rel_copy.start()
    load("wq").start()
    load("cot").start()
    load("wo").start()
    down_load(0).start()
    down_load(1).start()
    up_load(0).start()

    barrier = pltpu.get_barrier_semaphore()
    peers = place_peers[1:] + z_peers[1:] + [x_peer]
    for peer in peers:
        pl.semaphore_signal(barrier, inc=1, device_id=peer, device_id_type=MESH)
    pl.semaphore_wait(barrier, len(peers))

    def slices(i):
        return S[("wk", "wv")[i]].reshape(4, 2, 2, part_rows, width)

    def gather_x(i):
        source = (wk, wv)[i].at[pl.ds(pl.multiple_of(me * part_rows, 16), part_rows), :]
        return remote(source, slices(i).at[z, y, c], gxs.at[i], gxr.at[i], x_peer)

    def gather_z(i, k):
        own = slices(i).at[z, y, c]
        return remote(own, own, gzs.at[i, k - 1], gzr.at[i, k - 1], z_peers[k])

    def gather_z_here(i, k):
        found = slices(i).at[lax.rem(z + 4 - k, 4), y, c]
        return remote(found, found, gzs.at[i, k - 1], gzr.at[i, k - 1], z_peers[k])

    def gather_y(i, mine=True):
        held = slices(i).at[:, y if mine else 1 - y, c]
        return remote(held, held, gys.at[i], gyr.at[i], y_peer)

    def gather_core(i, mine=True):
        held = slices(i).at[:, :, c if mine else 1 - c]
        return remote(held, held, gcs.at[i], gcr.at[i], core_peer)

    gather_x(0).start()
    gather_x(1).start()

    def far_rows(part):
        return remote(
            slot("nt").at[:, span_of(part)],
            slot("ft").at[:, span_of(part)],
            xsem.at[part],
            xrem.at[part],
            x_peer,
        )

    load("x").wait()

    @unrolled_third
    def _(part, span):
        plain, inverse = plain_norm(W[0][span, :])
        low = (plain * gains[0:1, :] + shifts[0:1, :]).astype(bf16)
        S["nt"][:, span] = low.T
        far_rows(part).start()

    pltpu.make_async_copy(slot("nt"), nt_o, out_sem.at[2]).start()

    page_row = pages[...].astype(f32)
    side = st.astype(f32)
    valid_row = jnp.maximum(side, jnp.where(page_row < PAGES - 0.5, 1.0, 0.0))
    page_rows = [jnp.where(page_row == p, 1.0, 0.0) for p in range(PAGES)]
    for p in range(PAGES):
        page_low[p] = jnp.broadcast_to(page_rows[p], (size, slots)).astype(bf16)
    page_col[...] = jnp.broadcast_to(page_row, (128, slots)).T
    cell = lax.broadcasted_iota(jnp.int32, (GRID, third), 0)
    spot = lax.broadcasted_iota(jnp.int32, (GRID, third), 1)
    spot_first = jnp.where(lax.rem(spot, GRID) == cell, 1.0, 0.0)
    spot_second = jnp.where(lax.div(spot, GRID) == cell, 1.0, 0.0)
    spot_once = stack([spot_first, spot_second]).astype(bf16)
    spot_twice = stack([spot_once, spot_once])
    buckets = rel_table.shape[2] // 2
    radius = (buckets - 1) // 2
    toward = 1 - 2 * st
    cell = lax.broadcasted_iota(jnp.int32, (GRID, slots), 0)
    offsets = [
        jnp.clip(toward * (boxes[axis : axis + 1, :] - cell), -radius, radius) + radius
        for axis in range(2)
    ]

    rel_copy.wait()

    def bias_rows(head, carry):
        exact = []
        for axis in range(2):
            total = jnp.zeros((GRID, slots), f32)
            for bucket in range(buckets):
                total = jnp.where(
                    offsets[axis] == bucket, rel_table[head, 0, axis * buckets + bucket], total
                )
            total = total * LOG2E
            if axis == 0:
                total = jnp.where(page_row > PAGES - 0.5, masked_fill, total)
            exact.append(total)
        exact = stack(exact)
        high = exact.astype(bf16)
        bias[head, : 2 * GRID, :] = high
        bias[head, 2 * GRID :, :] = (exact - high.astype(f32)).astype(bf16)
        return carry

    lax.fori_loop(0, heads, bias_rows, 0)

    load("wq").wait()

    @unrolled_third
    def _(part, span):
        found = dot(S["wq"][:, span], S["nt"][...], "tn")
        S["q_t"][span, :] = (found * (LOG2E * size**-0.5)).astype(bf16)

    sums_o[...] = jnp.zeros_like(sums_o)
    late_o[...] = jnp.zeros_like(late_o)
    for i in range(2):
        gather_x(i).wait()
        for k in (1, 2, 3):
            gather_z(i, k).start()

    load("cot").wait()

    @unrolled_third
    def _(part, span):
        low = W[1][span, :].astype(bf16)
        S["g2"][span, :] = low
        sums_o[4:5, :] += jnp.sum(low.astype(f32), axis=0, keepdims=True)

    for t in range(4):
        down_load(t).wait()
        if t > 1:
            act_save(t - 2).wait()

        @unrolled_third
        def _(part, span):
            W[2 + t % 2][span, :] = dot(S["g2"][span, :], S["wd"][t % 2], "nt")

        act_save(t).start()
        down_load((t + 2) % 4).start()
        if t < 2:
            for k in (1, 2, 3):
                gather_z(t, k).wait_send()
                gather_z_here(t, k).wait_recv()
            gather_y(t).start()

    for i in range(2):
        gather_y(i).wait_send()
        gather_y(i, False).wait_recv()
        gather_core(i).start()

    for i, (weight, result) in enumerate((("wk", "k_t"), ("wv", "v_t"))):
        gather_core(i).wait_send()
        gather_core(i, False).wait_recv()

        @unrolled_third
        def _(part, span):
            if i == 0:
                far_rows(part).wait()
            S[result][:, span] = dot(S[weight][...], S["ft"][:, span], "tn").astype(bf16)

    act_save(2).wait()
    act_save(3).wait()
    act_load(0).start()

    def by_page(name, rows):
        return [S[name][rows, cols] for cols in thirds]

    def masked(name, rows):
        held = S[name][rows, :]
        return [held * page_low[p] for p in range(PAGES)]

    def fold(found):
        total = found[:size] * page_rows[0]
        for p in range(1, PAGES):
            total = total + found[p * size : (p + 1) * size] * page_rows[p]
        return total

    def column(p):
        return page_col[...] == p

    def spread(rows):
        middle, last = [jnp.concatenate([column(p)] * 2, axis=1) for p in (1, 2)]
        return jnp.where(middle, rows[1], jnp.where(last, rows[2], rows[0]))

    def rows_of(head):
        return pl.ds(pl.multiple_of(head * size, size), size)

    def in_pairs(step):
        def several(i, carry):
            for j in range(TOGETHER):
                step(TOGETHER * i + j, carry)
            return carry

        lax.fori_loop(0, heads // TOGETHER, several, 0)

    def text_forward(head, carry):
        rows = rows_of(head)
        scores = dot(
            stack(by_page("k_t", rows) + [spot_twice]),
            stack(masked("q_t", rows) + [bias[head]]),
            "tn",
        )
        top = jnp.max(scores, axis=0, keepdims=True)
        weight = jnp.exp2(scores - top).astype(bf16)
        found = dot(stack(by_page("v_t", rows) + [jnp.ones((16, third), bf16)]), weight)
        total = found[PAGES * size : PAGES * size + 1]
        S["att"][rows, :] = (fold(found) * (valid_row / total)).astype(bf16)
        lse[head] = top + jnp.log2(total)
        return carry

    def vision_forward(head, carry):
        rows = rows_of(head)
        scores = dot(
            stack(masked("k_t", rows) + [bias[head]]),
            stack(by_page("q_t", rows) + [spot_twice]),
            "tn",
        )
        tops = []
        for p in range(PAGES):
            inside = jnp.concatenate([column(p)] * 2, axis=1)
            tops.append(
                jnp.max(jnp.where(inside, scores, 2.0 * masked_fill), axis=0, keepdims=True)
            )
        weight = jnp.exp2(scores - spread(tops)).astype(bf16)
        counts = [page_low[p, :1, :] for p in range(PAGES)]
        counts = stack(counts + [jnp.zeros((16 - PAGES, slots), bf16)])
        found = dot(stack(masked("v_t", rows) + [counts]), weight)
        for p, cols in enumerate(thirds):
            total = found[PAGES * size + p : PAGES * size + p + 1]
            S["att"][rows, cols] = (found[p * size : (p + 1) * size] / total).astype(bf16)
            lse[head, :, cols] = tops[p] + jnp.log2(total)
        return carry

    @pl.when(st == 0)
    def _():
        in_pairs(text_forward)

    @pl.when(st == 1)
    def _():
        in_pairs(vision_forward)

    def down_view(at):
        return at.reshape(2, 2, width // 4, width)

    def rest_view(at):
        return at.reshape(4, 2, 2, part_rows, width)

    def add_low(left, right):
        return left + right

    def core_down(t):
        at = S["sd"].at[lax.rem(t, 2)]
        return remote(down_view(at).at[:, 1 - c], cd.at[t], csem.at[t], crem.at[t], core_peer)

    def core_rest(p, at):
        return remote(
            rest_view(at).at[:, :, 1 - c], cr.at[p], csem.at[4 + p], crem.at[4 + p], core_peer
        )

    def y_down(t):
        return remote(cd.at[t, 1 - y], yd.at[t], ysem.at[t], yrem.at[t], y_peer)

    def y_rest(p):
        return remote(cr.at[p, :, 1 - y], yr.at[p], ysem.at[4 + p], yrem.at[4 + p], y_peer)

    def z_down(t):
        return remote(yd.at[t], zd.at[t], zsem.at[0, t], zrem.at[0, t], z_peers[t + 1])

    def z_rest(p, i):
        q = chunk_of(p) if p < 4 else p
        return remote(
            yr.at[p, z_at[i]], zr.at[q, i - 1], zsem.at[1 + p, i - 1], zrem.at[1 + q, i - 1], z_peers[i]
        )

    def z_here(q, i):
        return remote(
            yr.at[q, z_at[i]], zr.at[q, i - 1], zsem.at[1 + q, i - 1], zrem.at[1 + q, i - 1], z_peers[i]
        )

    def after_core_down(t):
        core_down(t).wait()
        held = down_view(S["sd"].at[lax.rem(t, 2)])

        def part(i, carry):
            rows = pl.ds(pl.multiple_of(lax.rem(i, 2) * (2 * part_rows), 16), 2 * part_rows)
            j = lax.div(i, 2)
            cd[t, j, rows] = add_low(cd[t, j, rows], held[j, c, rows])
            return carry

        lax.fori_loop(0, 4, part, 0)
        y_down(t).start()

    def after_core(p, at):
        core_rest(p, at).wait()
        held = rest_view(at)

        def part(i, carry):
            cr[p, i] = add_low(cr[p, i], held[i, :, c])
            return carry

        lax.fori_loop(0, 4, part, 0)
        y_rest(p).start()

    def after_y_down(t):
        y_down(t).wait()

        def part(i, carry):
            rows = pl.ds(pl.multiple_of(i * (2 * part_rows), 16), 2 * part_rows)
            yd[t, rows] = add_low(yd[t, rows], cd[t, y, rows])
            return carry

        lax.fori_loop(0, 2, part, 0)
        if t < 3:
            z_down(t).start()

    def after_y(p):
        y_rest(p).wait()

        def part(i, carry):
            yr[p, i] = add_low(yr[p, i], cr[p, i, y])
            return carry

        lax.fori_loop(0, 4, part, 0)
        if p < 4:
            for i in (1, 2, 3):
                z_rest(p, i).start()
        else:
            z_near(p).start()

    def z_near(p):
        held = yr.at[p].reshape(2, 2, part_rows, width)
        return remote(
            held.at[:, 1 - z_low], zr.at[p, pl.ds(0, 2)], zsem.at[1 + p, 0], zrem.at[1 + p, 0], one_peer
        )

    def z_far(p):
        return remote(
            zr.at[p, 1 - z_high], zr.at[p, 2], zsem.at[1 + p, 1], zrem.at[1 + p, 1], two_peer
        )

    def after_near(p):
        z_near(p).wait()
        for i in range(2):
            zr[p, i] = add_low(zr[p, i], yr[p, 2 * i + z_low])
        z_far(p).start()

    def end_down():
        total = yd[3].astype(f32)
        for t in range(3):
            z_down(t).wait()
            total = total + zd[t].astype(f32)
        down_o[...] = total

    def end_rest(q):
        if q > 3:
            z_far(q).wait()
            return zr[q, z_high].astype(f32) + zr[q, 2].astype(f32)
        held = lax.rem(q - z + 3, 4) if q < 4 else q
        total = yr[held, z].astype(f32)
        for i in (1, 2, 3):
            z_here(q, i).wait()
            total = total + zr[q, i - 1].astype(f32)
        return total

    def exchange(mine, found, send, recv, peers, at, start):
        for k in (1, 2, 3):
            copy = remote(mine, found.at[at[0]], send.at[k - 1], recv.at[k - 1], peers[k])
            if start:
                copy.start()
            else:
                copy.wait_send()
                there = lax.rem(at[0] + 4 - k, 4)
                remote(mine, found.at[there], send.at[k - 1], recv.at[k - 1], peers[k]).wait_recv()
        if not start:
            found[at[0]] = mine[...]
            mine[...] = ((found[0] + found[1]) + found[2]) + found[3]

    def small_sums(stage, start):
        peers, at = ((place_peers, place_at), (z_peers, z_at))[stage]
        exchange(sums_o, sums_in.at[stage], asem.at[stage], arem.at[stage], peers, at, start)

    def small_table(stage, start):
        peers, at = ((place_peers, place_at), (z_peers, z_at))[stage]
        exchange(table_o, table_in.at[stage], bsem.at[stage], brem.at[stage], peers, at, start)

    pltpu.make_async_copy(slot("nt"), nt_o, out_sem.at[2]).wait()
    load("wo").wait()

    @unrolled_third
    def _(part, span):
        middle = W[0][span, :] + dot(S["att"][:, span], S["wo"][...], "tn")
        W[0][span, :] = middle
        W[2][span, :] = middle + down_bias[...]
        W[3][span, :] = jnp.zeros((third, width), f32)
        plain, inverse = plain_norm(middle)
        S["n2"][span, :] = (plain * gains[1:2, :] + shifts[1:2, :]).astype(bf16)

    def feed(t, carry):
        two = lax.rem(t, 2)
        at = chunk_of(t)
        up_load(t).wait()
        down_load(t).wait()
        act_load(t).wait()

        @pl.when(t < 3)
        def _():
            up_load(t + 1).start()

            @pl.when(t > 0)
            def _():
                down_load(t + 1).start()

        w_u = S["wu"].at[two]
        w_d = S["wd"].at[two]

        @unrolled_third
        def _(part, cols):
            pre = dot(S["n2"][...], w_u[:, cols]) + up_bias[at, :, cols]
            square = pre * pre
            gate = jnp.tanh(pre * (GELU_IN + (GELU_IN * GELU_CUBE) * square))
            gate_half = 0.5 + 0.5 * gate
            act = (pre * gate_half).astype(bf16)
            S["act"][:, cols] = act
            S["sd"][two, cols, :] = dot(act, S["g2"][...], "tn").astype(bf16)
            slope = pre * (GELU_IN + (3.0 * GELU_IN * GELU_CUBE) * square)
            grad_act = W[1][:, cols]
            grad_pre = (grad_act * (gate_half * (1.0 + (1.0 - gate) * slope))).astype(bf16)
            S["gp"][:, cols] = grad_pre
            sums_o[pl.ds(5 + at, 1), cols] = jnp.sum(grad_pre.astype(f32), axis=0, keepdims=True)

        @pl.when(t < 3)
        def _():
            act_load(t + 1).start()

        @pl.when(t == 3)
        def _():
            load("cot").start()

        core_down(t).start()

        @unrolled_third
        def _(part, cols):
            S["sr"][two, :, cols] = dot(S["n2"][...], S["gp"][:, cols], "tn").astype(bf16)

        core_rest(t, S["sr"].at[two]).start()
        after_core_down(t)

        @pl.when(t > 0)
        def _():
            after_core(t - 1, S["sr"].at[1 - two])

        @unrolled_third
        def _(part, span):
            W[2][span, :] = W[2][span, :] + dot(S["act"][span, :], w_d[...])
            W[3][span, :] = W[3][span, :] + dot(S["gp"][span, :], w_u[...], "nt")

        @pl.when(t == 1)
        def _():
            after_y_down(0)

        @pl.when(t == 2)
        def _():
            after_y(0)

        @pl.when(t == 3)
        def _():
            after_y_down(1)

        return carry

    lax.fori_loop(0, 4, feed, 0)
    after_core(3, S["sr1"])
    load("cot").wait()

    pltpu.make_async_copy(W[2], block_o, out_sem.at[0]).start()

    @unrolled_third
    def _(part, span):
        plain, inverse = plain_norm(W[0][span, :])
        grad_two = W[3][span, :]
        sums_o[1:2, :] += jnp.sum(grad_two * plain, axis=0, keepdims=True)
        sums_o[3:4, :] += jnp.sum(grad_two, axis=0, keepdims=True)
        middle = W[1][span, :] + norm_backward(grad_two, plain, inverse, gains[1:2, :])
        W[0][span, :] = middle
        S["gm"][span, :] = middle.astype(bf16)

    load("x_again").start()
    load("wq_again").start()
    load("nt_again").start()

    @unrolled_third
    def _(part, rows):
        grad_att = (dot(S["wo"][rows, :], S["gm"][...], "nt") * valid_row).astype(bf16)
        S["go"][rows, :] = grad_att
        both = S["att"][rows, :].astype(f32) * grad_att.astype(f32)
        delta[pl.ds(4 * part, 4)] = jnp.sum(both.reshape(4, size, slots), axis=1, keepdims=True)

    after_y(1)

    def table_rows(head, found):
        for axis in range(2):
            here = found[axis * GRID : (axis + 1) * GRID]
            for bucket in range(buckets):
                kept = jnp.where(offsets[axis] == bucket, here, 0.0)
                cells[pl.ds(head * 16 + axis * buckets + bucket, 1), :] = jnp.sum(
                    kept, axis=0, keepdims=True
                )

    def text_backward(head, carry):
        rows = rows_of(head)
        keys = by_page("k_t", rows)
        queries = masked("q_t", rows)
        grads = stack(masked("go", rows))
        scores = dot(stack(keys + [spot_twice]), stack(queries + [bias[head]]), "tn")
        prob = jnp.exp2(scores - lse[head])
        grad_prob = dot(stack(by_page("v_t", rows)), grads, "tn")
        grad_score = (prob * (grad_prob - delta[head])).astype(bf16)
        found = dot(grads, prob.astype(bf16), "nt")
        for p, cols in enumerate(thirds):
            S["dv"][rows, cols] = found[p * size : (p + 1) * size].astype(bf16)
        found = dot(stack(queries), grad_score, "nt") * LN2
        for p, cols in enumerate(thirds):
            S["dk"][rows, cols] = found[p * size : (p + 1) * size].astype(bf16)
        found = dot(stack(keys + [spot_once]), grad_score)
        S["dq"][rows, :] = (fold(found) * size**-0.5).astype(bf16)
        table_rows(head, found[PAGES * size :])
        return carry

    def vision_backward(head, carry):
        rows = rows_of(head)
        keys = masked("k_t", rows)
        queries = by_page("q_t", rows)
        grads = stack(by_page("go", rows))
        scores = dot(stack(keys + [bias[head]]), stack(queries + [spot_twice]), "tn")
        prob = jnp.exp2(scores - spread([lse[head, :, cols] for cols in thirds]))
        grad_prob = dot(stack(masked("v_t", rows)), grads, "tn")
        inner = spread([delta[head, :, cols] for cols in thirds])
        grad_score = (prob * (grad_prob - inner)).astype(bf16)
        S["dv"][rows, :] = fold(dot(grads, prob.astype(bf16), "nt")).astype(bf16)
        found = dot(stack(queries + [spot_once]), grad_score, "nt")
        S["dk"][rows, :] = (fold(found) * LN2).astype(bf16)
        table_rows(head, found[PAGES * size :])
        found = dot(stack(keys), grad_score) * size**-0.5
        for p, cols in enumerate(thirds):
            S["dq"][rows, cols] = found[p * size : (p + 1) * size].astype(bf16)
        return carry

    cells[...] = jnp.zeros_like(cells)

    @pl.when(st == 0)
    def _():
        in_pairs(text_backward)

    @pl.when(st == 1)
    def _():
        in_pairs(vision_backward)

    after_y_down(2)

    load("x_again").wait()
    base = heads * 16
    cells[base + 2 : base + 3, :] = valid_row

    @unrolled_third
    def _(part, span):
        block = W[2][span, :]
        own = jnp.maximum(side, jnp.where(page_col[span, 0:1] < PAGES - 0.5, 1.0, 0.0))
        sub = block - W[3][span, :]
        cells[base : base + 1, :] += jnp.sum(own * block * block, axis=0, keepdims=True)
        cells[base + 1 : base + 2, :] += jnp.sum(own * sub * sub, axis=0, keepdims=True)

    table_o[...] = lax.dot_general(
        jnp.ones((8, width), f32),
        cells[...],
        (((1,), (1,)), ((), ())),
        preferred_element_type=f32,
        precision=lax.Precision.HIGHEST,
    )

    small_sums(0, True)
    small_table(0, True)

    def back_rows(part):
        return remote(
            slot("send").at[:, span_of(part)],
            slot("back").at[:, span_of(part)],
            xsem.at[3 + part],
            xrem.at[3 + part],
            x_peer,
        )

    @unrolled_third
    def _(part, cols):
        S["send"][:, cols] = (
            dot(S["wk"][...], S["dk"][:, cols])
            + dot(S["wv"][...], S["dv"][:, cols])
        ).astype(bf16)
        back_rows(part).start()


    @unrolled_third
    def _(part, span):
        S["sk"][span, :] = dot(S["ft"][span, :], S["dk"][...], "nt").astype(bf16)

    core_rest(5, S["sk"]).start()
    after_y(2)

    @unrolled_third
    def _(part, span):
        S["sv"][span, :] = dot(S["ft"][span, :], S["dv"][...], "nt").astype(bf16)

    core_rest(6, S["sv"]).start()
    after_core(5, S["sk"])

    @unrolled_third
    def _(part, span):
        S["so"][span, :] = dot(S["att"][span, :], S["gm"][...]).astype(bf16)

    core_rest(4, S["so"]).start()
    after_core(6, S["sv"])
    load("nt_again").wait()

    @unrolled_third
    def _(part, span):
        S["sq"][span, :] = dot(S["nt_again"][span, :], S["dq"][...], "nt").astype(bf16)

    core_rest(7, S["sq"]).start()
    after_core(4, S["so"])
    load("wq_again").wait()

    @unrolled_third
    def _(part, span):
        W[1][span, :] = dot(S["wq_again"][span, :], S["dq"][...])

    after_core(7, S["sq"])
    after_y_down(3)

    def last_small(stage, start):
        peers, at = ((place_peers, place_at), (z_peers, z_at))[stage]
        exchange(late_o, late_in.at[stage], lsem.at[stage], lrem.at[stage], peers, at, start)

    table_swap = remote(table_o, table_far, tsem, trem, x_peer)

    def hop_copy(i):
        return remote(hop.at[i], hop_in.at[i], hsem.at[i], hrem.at[i], x_peer)

    after_y(3)
    pltpu.make_async_copy(W[2], block_o, out_sem.at[0]).wait()

    @each_third
    def _(part, span):
        back_rows(part).wait()
        grad_one = (W[1][:, span] + S["back"][:, span].astype(f32)).T
        plain, inverse = plain_norm(W[3][span, :])
        late_o[0:1, :] += jnp.sum(grad_one * plain, axis=0, keepdims=True)
        late_o[1:2, :] += jnp.sum(grad_one, axis=0, keepdims=True)
        W[2][span, :] = W[0][span, :] + norm_backward(
            grad_one, plain, inverse, gains[0:1, :]
        )

        @pl.when(part == 0)
        def _():
            small_sums(0, False)
            small_sums(1, True)
            small_table(0, False)
            small_table(1, True)

        @pl.when(part == 1)
        def _():
            after_y(5)

    pltpu.make_async_copy(W[2], grad_o, out_sem.at[1]).start()
    last_small(0, True)
    after_near(5)
    after_y(6)
    end_down()
    for q in range(4):
        up_o[:, q * width : (q + 1) * width] = end_rest(q)
    after_y(4)
    after_near(6)
    small_sums(1, False)
    small_table(1, False)
    table_swap.start()
    hop[0] = end_rest(5).astype(bf16)
    hop_copy(0).start()
    last_small(0, False)
    last_small(1, True)
    after_near(4)
    after_y(7)
    hop[1] = end_rest(6).astype(bf16)
    hop_copy(1).start()
    wo_o[...] = end_rest(4)
    after_near(7)
    last_small(1, False)
    wq_o[...] = end_rest(7)
    table_swap.wait()
    lane = lax.broadcasted_iota(jnp.int32, table_o.shape, 1)
    table_o[...] = table_o[...] + jnp.where(lane >= base, table_far[...], 0.0)
    for i in range(2):
        hop_copy(i).wait()
        hop_o[i] = hop_in[i].astype(f32)
    pltpu.make_async_copy(W[2], grad_o, out_sem.at[1]).wait()


def hand_over(
    block, grad_in, down, up, out, query, hop, sums, late, table,
    block_o, grad_o, gains_o, shifts_o, query_o, key_o, value_o, out_o, up_o, up_bias_o, down_o, down_bias_o, table_o, stats_o,
    held, down_h, up_h, out_h, query_h, hop_h, sums_h, late_h, table_h, in_sem, out_sem, sem,
):
    slots, width = block.shape
    step = slots // 4
    moves = []
    for i, (source, target) in enumerate(((block, block_o), (grad_in, grad_o))):
        for j in range(4):
            span = pl.ds(j * step, step)
            moves.append(
                (
                    pltpu.make_async_copy(
                        source.at[span, :], held.at[i, span, :], in_sem.at[i, j]
                    ),
                    pltpu.make_async_copy(
                        held.at[i, span, :], target.at[span, :], out_sem.at[i, j]
                    ),
                )
            )
    for i, (source, kept, target) in enumerate(((down, down_h, down_o), (up, up_h, up_o))):
        moves.append(
            (
                pltpu.make_async_copy(source, kept, sem.at[i]),
                pltpu.make_async_copy(kept, target, sem.at[i + 8]),
            )
        )
    small = ((out, out_h), (query, query_h), (hop, hop_h), (sums, sums_h), (late, late_h), (table, table_h))
    small = [pltpu.make_async_copy(*pair, sem.at[i + 2]) for i, pair in enumerate(small)]
    for copy in small:
        copy.start()
    for move in moves:
        move[0].start()
    for copy in small:
        copy.wait()
    gains_o[0:1, :] = late_h[0:1, :]
    gains_o[1:2, :] = sums_h[1:2, :]
    shifts_o[0:1, :] = late_h[1:2, :]
    shifts_o[1:2, :] = sums_h[3:4, :]
    down_bias_o[...] = sums_h[4:5, :]
    for q in range(4):
        up_bias_o[:, q * width : (q + 1) * width] = sums_h[5 + q : 6 + q, :]
    query_o[...] = query_h[...]
    key_o[...] = hop_h[0]
    value_o[...] = hop_h[1]
    out_o[...] = out_h[...]
    heads, _, rows = table_o.shape
    for head in range(heads):
        table_o[head] = table_h[0:1, head * 16 : head * 16 + rows]
    total = table_h[0:1, heads * 16 : heads * 16 + 2]
    count = table_h[0:1, heads * 16 + 2 : heads * 16 + 3]
    stats_o[...] = jnp.sqrt(total / (count * width))
    for move in moves:
        move[0].wait()
        move[1].start()
    for move in moves:
        move[1].wait()


def on_device(
    inputs,
    text_pages,
    text_boxes,
    norm_gains,
    norm_shifts,
    w_query,
    w_key,
    w_value,
    w_out,
    w_up,
    up_bias,
    w_down,
    down_bias,
    box_table,
    cotangent,
):
    slots, width = inputs.shape[2:]
    rel_rows, heads = box_table.shape[1:]
    size = width // heads
    part = width // 16
    shape = lambda *dims: jax.ShapeDtypeStruct(dims, f32)
    vmem = pl.BlockSpec(memory_space=pltpu.VMEM)
    hbm = pl.BlockSpec(memory_space=pl.ANY)
    dma = pltpu.SemaphoreType.DMA
    cell_rows = heads * 16 + 16
    low = lambda *dims: pltpu.VMEM(dims, bf16)
    full = lambda *dims: pltpu.VMEM(dims, f32)
    block, grad_in, _, _, down, up, out, query, hop, sums, late, table = pl.pallas_call(
        layer_kernel,
        out_shape=[
            shape(slots, width),
            shape(slots, width),
            jax.ShapeDtypeStruct((width, slots), bf16),
            shape(4, slots, width),
            shape(4 * part, width),
            shape(part, 4 * width),
            shape(part, width),
            shape(part, width),
            shape(2, part, width),
            shape(16, width),
            shape(8, width),
            shape(8, cell_rows),
        ],
        in_specs=[hbm] * 8 + [vmem] * 6 + [hbm],
        out_specs=[hbm] * 4 + [vmem] * 8,
        scratch_shapes=[
            [low(slots, width)] * (len(NAMES) - RINGS) + [low(2, slots, width)] * RINGS,
            [full(slots, width)] * 4,
            pltpu.SMEM((heads, 1, rel_rows), f32),
            low(heads, 4 * GRID, slots),
            full(heads, 1, slots),
            full(heads, 1, slots),
            low(PAGES, size, slots),
            full(slots, 128),
            full(cell_rows, width),
            low(4, 2, 4 * part, width),
            low(8, 4, 2, part, width),
            low(4, 4 * part, width),
            low(8, 4, part, width),
            low(3, 4 * part, width),
            low(8, 3, part, width),
            low(2, part, width),
            low(2, part, width),
            full(2, 4, 16, width),
            full(2, 4, 8, width),
            full(2, 4, 8, cell_rows),
            full(8, cell_rows),
            dma((7,)),
            dma((3, 3)),
            dma((3,)),
            dma((12,)),
            dma((12,)),
            dma((12,)),
            dma((12,)),
            dma((9, 3)),
            dma((9, 3)),
            dma((6,)),
            dma((6,)),
            dma((2,)),
            dma((2,)),
            dma((2, 3)),
            dma((2, 3)),
            dma((2, 3)),
            dma((2, 3)),
            dma((2, 3)),
            dma((2, 3)),
            dma,
            dma,
            dma((2,)),
            dma((2,)),
            dma((2, 3)),
            dma((2, 3)),
            dma((2,)),
            dma((2,)),
            dma((2,)),
            dma((2,)),
        ],
        compiler_params=pltpu.CompilerParams(
            collective_id=0, has_side_effects=True, vmem_limit_bytes=61 * 2**20
        ),
        name="layer",
    )(
        inputs[0, 0],
        cotangent[0, 0],
        w_query[0],
        w_key[0],
        w_value[0],
        w_out[0],
        w_up[0],
        w_down[0],
        up_bias.reshape(4, 1, width),
        down_bias,
        norm_gains[0],
        norm_shifts[0],
        text_pages,
        text_boxes[0],
        box_table.transpose(2, 0, 1),
    )
    outs = pl.pallas_call(
        hand_over,
        out_shape=[
            shape(slots, width),
            shape(slots, width),
            shape(2, width),
            shape(2, width),
            shape(part, width),
            shape(part, width),
            shape(part, width),
            shape(part, width),
            shape(part, 4 * width),
            shape(1, 4 * width),
            shape(4 * part, width),
            shape(1, width),
            shape(heads, 1, rel_rows),
            shape(1, 2),
        ],
        in_specs=[hbm] * 10,
        out_specs=[hbm] * 2 + [vmem] * 6 + [hbm, vmem, hbm] + [vmem] * 3,
        scratch_shapes=[
            full(2, slots, width),
            full(4 * part, width),
            full(part, 4 * width),
            full(part, width),
            full(part, width),
            full(2, part, width),
            full(16, width),
            full(8, width),
            full(8, cell_rows),
            dma((2, 4)),
            dma((2, 4)),
            dma((10,)),
        ],
        compiler_params=pltpu.CompilerParams(vmem_limit_bytes=61 * 2**20),
        name="hand_over",
    )(block, grad_in, down, up, out, query, hop, sums, late, table)
    block, grad_in, gains, shifts, query, key, value, out, up, up_b, down, down_b, table, stats = outs
    return (
        block[None, None],
        grad_in[None, None],
        gains[None],
        shifts[None],
        query[None],
        key[None],
        value[None],
        out[None],
        up[None],
        up_b,
        down[None],
        down_b,
        table.transpose(1, 2, 0),
        stats[0],
    )


def partner(block, axis, bit):
    count = lax.axis_size(axis)
    route = []
    for low in range(count):
        high = low | 1 << bit
        if high != low and high < count:
            route += [(low, high), (high, low)]
    return lax.ppermute(block, axis, route)


def norm_forward(values, gain_row, shift_row):
    center = values - jnp.mean(values, axis=-1, keepdims=True)
    inverse = lax.rsqrt(jnp.mean(center * center, axis=-1, keepdims=True) + 1e-05)
    normal_part = center * inverse
    return (normal_part * gain_row + shift_row, normal_part, inverse)


def general_norm_backward(grad_normed, normal_part, inverse, gain_row):
    scaled = grad_normed * gain_row
    first_mean = jnp.mean(scaled, axis=-1, keepdims=True)
    second_mean = jnp.mean(scaled * normal_part, axis=-1, keepdims=True)
    return inverse * (scaled - first_mean - normal_part * second_mean)


def bucket_offset(own_coord, far_coord, bucket_count):
    radius = (bucket_count - 1) // 2
    return jnp.clip(own_coord[:, None] - far_coord[None, :], -radius, radius) + radius


def bias_from(rel_table, offset):
    result = jnp.zeros((rel_table.shape[1],) + offset.shape, f32)
    for bucket in range(rel_table.shape[0]):
        result = (
            result + rel_table[bucket][:, None, None] * (offset == bucket).astype(f32)[None]
        )
    return result


def bias_grad(grad_wide, offset, bucket_count):
    return jnp.stack(
        [
            jnp.sum(grad_wide * (offset == bucket).astype(f32)[None], axis=(1, 2))
            for bucket in range(bucket_count)
        ]
    )


def project(left, right):
    return jnp.einsum("rsd,de->rse", left, right, preferred_element_type=f32)


def weight_grad(left, right):
    return jnp.einsum("rsd,rse->de", left, right, preferred_element_type=f32)


def back_project(grad_low, weight):
    return jnp.einsum("rse,de->rsd", grad_low, weight, preferred_element_type=f32)


def general_device(
    inputs,
    text_pages,
    text_boxes,
    norm_gains,
    norm_shifts,
    w_query,
    w_key,
    w_value,
    w_out,
    w_up,
    up_bias,
    w_down,
    down_bias,
    box_table,
    cotangent,
):
    slot_count = inputs.shape[2]
    model_width = inputs.shape[3]
    head_count = box_table.shape[2]
    head_size = model_width // head_count
    bucket_count = box_table.shape[1] // 2
    score_scale = head_size ** (-0.5)
    is_text = lax.axis_index("stream") == 0
    positions = jnp.arange(slot_count, dtype=jnp.int32)
    cell_index = positions % (GRID * GRID)
    vision_page = positions // (GRID * GRID)
    vision_first = cell_index % GRID
    vision_second = cell_index // GRID
    own_valid = jnp.where(is_text, text_pages < PAGES, True).astype(f32)
    gain_rows = norm_gains[0]
    shift_rows = norm_shifts[0]
    rel_table = box_table[0]
    block_in = inputs[:, 0]
    normed_one, plain_one, inverse_one = norm_forward(block_in, gain_rows[0], shift_rows[0])
    normed_low = normed_one.astype(bf16)
    query = project(normed_low, w_query[0]).astype(bf16)
    own_keys = project(normed_low, w_key[0]).astype(bf16)
    own_values = project(normed_low, w_value[0]).astype(bf16)
    far_keys, far_values = partner((own_keys, own_values), "stream", 0)

    def geometry(row_index):
        text_page = text_pages[row_index]
        own_page = jnp.where(is_text, text_page, vision_page)
        far_page = jnp.where(is_text, vision_page, text_page)
        own_first = jnp.where(is_text, text_boxes[row_index, 0], vision_first)
        far_first = jnp.where(is_text, vision_first, text_boxes[row_index, 0])
        own_second = jnp.where(is_text, text_boxes[row_index, 1], vision_second)
        far_second = jnp.where(is_text, vision_second, text_boxes[row_index, 1])
        allowed = (own_page[:, None] == far_page[None, :]) | (own_page[:, None] == PAGES)
        return (
            allowed,
            bucket_offset(own_first, far_first, bucket_count),
            bucket_offset(own_second, far_second, bucket_count),
        )

    def heads_of(matrix):
        return matrix.reshape(slot_count, head_count, head_size)

    def score_block(row_index, allowed, offset_first, offset_second):
        raw = (
            jnp.einsum(
                "ihd,jhd->hij",
                heads_of(query[row_index]),
                heads_of(far_keys[row_index]),
                preferred_element_type=f32,
            )
            * score_scale
        )
        raw = (
            raw
            + bias_from(rel_table[:bucket_count], offset_first)
            + bias_from(rel_table[bucket_count:], offset_second)
        )
        return jnp.where(allowed[None], raw, masked_fill)

    row_index = 0
    allowed, offset_first, offset_second = geometry(row_index)
    masked = score_block(row_index, allowed, offset_first, offset_second)
    top_score = jnp.max(masked, axis=-1, keepdims=True)
    exp_scores = jnp.exp(masked - top_score)
    row_total = jnp.sum(exp_scores, axis=-1, keepdims=True)
    prob_low = (exp_scores / row_total).astype(bf16)
    attended = jnp.einsum(
        "hij,jhd->ihd",
        prob_low,
        heads_of(far_values[row_index]),
        preferred_element_type=f32,
    ).reshape(slot_count, model_width)
    attended_rows = [(attended * own_valid[row_index][:, None]).astype(bf16)]
    log_totals = [top_score + jnp.log(row_total)]
    attended_low = jnp.stack(attended_rows)
    branch_one = project(attended_low, w_out[0])
    middle = block_in + branch_one
    normed_two, plain_two, inverse_two = norm_forward(middle, gain_rows[1], shift_rows[1])
    normed_two_low = normed_two.astype(bf16)
    pre_act = project(normed_two_low, w_up[0]) + up_bias[0]
    act_low = jax.nn.gelu(pre_act).astype(bf16)
    branch_two = project(act_low, w_down[0]) + down_bias[0]
    block_out = middle + branch_two
    sublayer = branch_one + branch_two
    totals = lax.psum(
        (
            jnp.sum(own_valid * jnp.sum(block_out * block_out, axis=-1)),
            jnp.sum(own_valid * jnp.sum(sublayer * sublayer, axis=-1)),
            jnp.sum(own_valid),
        ),
        ("stream", "batch"),
    )
    denominator = totals[2] * model_width
    stats = jnp.stack([jnp.sqrt(totals[0] / denominator), jnp.sqrt(totals[1] / denominator)])
    grad_out = cotangent[:, 0]
    grad_out_low = grad_out.astype(bf16)
    grad_w_down = weight_grad(act_low, grad_out_low)
    grad_down_bias = jnp.sum(grad_out_low.astype(f32), axis=(0, 1))
    grad_act = back_project(grad_out_low, w_down[0])
    gelu_back = jax.vjp(jax.nn.gelu, pre_act)[1]
    grad_pre_low = gelu_back(grad_act)[0].astype(bf16)
    grad_w_up = weight_grad(normed_two_low, grad_pre_low)
    grad_up_bias = jnp.sum(grad_pre_low.astype(f32), axis=(0, 1))
    grad_normed_two = back_project(grad_pre_low, w_up[0])
    grad_gain_two = jnp.sum(grad_normed_two * plain_two, axis=(0, 1))
    grad_shift_two = jnp.sum(grad_normed_two, axis=(0, 1))
    grad_middle = grad_out + general_norm_backward(grad_normed_two, plain_two, inverse_two, gain_rows[1])
    grad_middle_low = grad_middle.astype(bf16)
    grad_w_out = weight_grad(attended_low, grad_middle_low)
    grad_attended = back_project(grad_middle_low, w_out[0]).astype(bf16) * own_valid[
        :, :, None
    ].astype(bf16)
    query_grad_rows, key_grad_rows, value_grad_rows = ([], [], [])
    row_index = 0
    allowed, offset_first, offset_second = geometry(row_index)
    masked = score_block(row_index, allowed, offset_first, offset_second)
    prob = jnp.exp(masked - log_totals[row_index])
    grad_heads = heads_of(grad_attended[row_index])
    grad_prob = jnp.einsum(
        "ihd,jhd->hij",
        grad_heads,
        heads_of(far_values[row_index]),
        preferred_element_type=f32,
    )
    inner_sum = jnp.sum(prob * grad_prob, axis=-1, keepdims=True)
    grad_score_low = (prob * (grad_prob - inner_sum)).astype(bf16)
    grad_score_wide = grad_score_low.astype(f32)
    grad_table = jnp.concatenate(
        [
            bias_grad(grad_score_wide, offset_first, bucket_count),
            bias_grad(grad_score_wide, offset_second, bucket_count),
        ],
        axis=0,
    )
    query_grad = (
        jnp.einsum(
            "hij,jhd->ihd",
            grad_score_low,
            heads_of(far_keys[row_index]),
            preferred_element_type=f32,
        )
        * score_scale
    )
    key_grad = (
        jnp.einsum(
            "hij,ihd->jhd",
            grad_score_low,
            heads_of(query[row_index]),
            preferred_element_type=f32,
        )
        * score_scale
    )
    value_grad = jnp.einsum(
        "hij,ihd->jhd", prob.astype(bf16), grad_heads, preferred_element_type=f32
    )
    query_grad_rows.append(query_grad.reshape(slot_count, model_width).astype(bf16))
    key_grad_rows.append(key_grad.reshape(slot_count, model_width).astype(bf16))
    value_grad_rows.append(value_grad.reshape(slot_count, model_width).astype(bf16))
    grad_query_low = jnp.stack(query_grad_rows)
    own_key_grad, own_value_grad = partner(
        (jnp.stack(key_grad_rows), jnp.stack(value_grad_rows)), "stream", 0
    )
    grad_w_query = weight_grad(normed_low, grad_query_low)
    grad_w_key = weight_grad(normed_low, own_key_grad)
    grad_w_value = weight_grad(normed_low, own_value_grad)
    grad_normed_one = (
        back_project(grad_query_low, w_query[0])
        + back_project(own_key_grad, w_key[0])
        + back_project(own_value_grad, w_value[0])
    )
    grad_gain_one = jnp.sum(grad_normed_one * plain_one, axis=(0, 1))
    grad_shift_one = jnp.sum(grad_normed_one, axis=(0, 1))
    grad_inputs = grad_middle + general_norm_backward(grad_normed_one, plain_one, inverse_one, gain_rows[0])
    big_sums = (
        lax.psum_scatter(grad_w_query, "batch", scatter_dimension=0, tiled=True),
        lax.psum_scatter(grad_w_key, "batch", scatter_dimension=0, tiled=True),
        lax.psum_scatter(grad_w_value, "batch", scatter_dimension=0, tiled=True),
        lax.psum_scatter(grad_w_out, "batch", scatter_dimension=0, tiled=True),
        lax.psum_scatter(grad_w_up, "batch", scatter_dimension=0, tiled=True),
        lax.psum_scatter(grad_w_down, "batch", scatter_dimension=0, tiled=True),
    )
    small_sums = lax.psum(
        (
            jnp.stack([grad_gain_one, grad_gain_two]),
            jnp.stack([grad_shift_one, grad_shift_two]),
            grad_up_bias,
            grad_down_bias,
            grad_table,
        ),
        "batch",
    )
    return (
        block_out[:, None],
        grad_inputs[:, None],
        small_sums[0][None],
        small_sums[1][None],
        big_sums[0][None],
        big_sums[1][None],
        big_sums[2][None],
        big_sums[3][None],
        big_sums[4][None],
        small_sums[2][None],
        big_sums[5][None],
        small_sums[3][None],
        small_sums[4][None],
        stats,
    )


def solution(mesh):
    sided = lambda dims: P("stream", *([None] * (dims - 1)))
    rows = P("batch", "stream", None, None)
    shard = P("stream", "batch", None)
    placed = (
        (rows, P("batch", None), P("batch", None, None), sided(3), sided(3))
        + (sided(3),) * 5
        + (sided(2), sided(3), sided(2), sided(3), rows)
    )
    fits = mesh.shape["batch"] == 16 and mesh.shape["stream"] == 2
    return jax.shard_map(
        on_device if fits else general_device,
        mesh=mesh,
        in_specs=placed,
        out_specs=(
            (rows, rows, sided(3), sided(3))
            + (shard,) * 5
            + (sided(2), shard, sided(2), sided(3), P())
        ),
        check_vma=False,
    )
```

profile of v0, /device:TPU:0, one launch (start us, length us, event | category | flops | bytes accessed | tf_op | source)
XLA Modules:
  0.0 170.0 jit_solution(14730251082955358623)
XLA Ops:
  0.7 163.5 %layer.1 = (f32[768,768]{1,0:T(8,128)}, f32[768,768]{1,0:T(8,128)}, bf16[768,768]{1,0:T(8,128)(2,1)}, f32[4,768,768]{2,1,0:T(8,128)}, f32[192,768]{1,0:T(8,128)}...) custom-call(f32[768,768]{1,0:T(8,128)} %bitcast.27, ...), custom_call_target="tpu_custom_call" | custom-call | tf_op jit(solution)/shard_map/layer/pallas_call | solution.py:941
  164.1 5.6 %hand_over.1 = (f32[768,768]{1,0:T(8,128)}, f32[768,768]{1,0:T(8,128)}, f32[2,768]{1,0:T(2,128)}, f32[2,768]{1,0:T(2,128)}, f32[48,768]{1,0:T(8,128)}, /*index=5...) custom-call(f32[768,768]{1,0:T(8,128)} %get-tuple-element.38.block, ...), custom_call_target="tpu_custom_call" | custom-call | tf_op jit(solution)/shard_map/hand_over/pallas_call | solution.py:1032
where the time goes:
time: 172 us; the launch traced here: 170 us
  Pallas kernels  169 us (98%)
    pallas_call x1, Pallas kernels, on_device(): pl.pallas_call(layer_kernel, out_shape=[shape(slots, width), shape(slots,...  163 us
    pallas_call x1, Pallas kernels, on_device(): pl.pallas_call(hand_over, out_shape=[shape(slots, width), shape(slots, wi...  5.62 us

commit v1 on v0

--- a/solution.py
+++ b/solution.py
@@ -115,7 +115,7 @@
         )
 
     singles = dict(
-        x=(x, W[0]), cot=(cot, W[1]), wo=(wo, slot("wo")), wq=(wq, slot("wq")),
+        cot=(cot, W[1]), wo=(wo, slot("wo")), wq=(wq, slot("wq")),
         x_again=(x, W[3]), wq_again=(wq, slot("wq_again")), nt_again=(nt_o, slot("nt_again")),
     )
     load_at = {name: i for i, name in enumerate(singles)}
@@ -146,7 +146,12 @@
     def act_save(t):
         return pltpu.make_async_copy(W[2 + t % 2], ga_o.at[t], w_sem.at[2, 1 + t % 2])
 
-    load("x").start()
+    def first_rows(part):
+        span = span_of(part)
+        return pltpu.make_async_copy(x.at[span, :], W[0].at[span, :], w_sem.at[3, part])
+
+    for part in range(3):
+        first_rows(part).start()
     rel_copy = pltpu.make_async_copy(rel_hbm, rel_table, out_sem.at[1])
     rel_copy.start()
     load("wq").start()
@@ -197,10 +202,10 @@
             x_peer,
         )
 
-    load("x").wait()
 
     @unrolled_third
     def _(part, span):
+        first_rows(part).wait()
         plain, inverse = plain_norm(W[0][span, :])
         low = (plain * gains[0:1, :] + shifts[0:1, :]).astype(bf16)
         S["nt"][:, span] = low.T
@@ -979,7 +984,7 @@
             full(2, 4, 8, cell_rows),
             full(8, cell_rows),
             dma((7,)),
-            dma((3, 3)),
+            dma((4, 3)),
             dma((3,)),
             dma((12,)),
             dma((12,)),

time: 172 us -> 172 us (level)
  no operation moved by 1% of the time
where the time goes in v1:
time: 172 us; the launch traced here: 170 us
  Pallas kernels  169 us (98%)
    pallas_call x1, Pallas kernels, on_device(): pl.pallas_call(layer_kernel, out_shape=[shape(slots, width), shape(slots,...  163 us
    pallas_call x1, Pallas kernels, on_device(): pl.pallas_call(hand_over, out_shape=[shape(slots, width), shape(slots, wi...  5.62 us

profile of v1, /device:TPU:0, one launch (start us, length us, event | category | flops | bytes accessed | tf_op | source)
XLA Modules:
  0.0 170.0 jit_solution(6762079327094671901)
XLA Ops:
  0.7 163.5 %layer.1 = (f32[768,768]{1,0:T(8,128)}, f32[768,768]{1,0:T(8,128)}, bf16[768,768]{1,0:T(8,128)(2,1)}, f32[4,768,768]{2,1,0:T(8,128)}, f32[192,768]{1,0:T(8,128)}...) custom-call(f32[768,768]{1,0:T(8,128)} %bitcast.27, ...), custom_call_target="tpu_custom_call" | custom-call | tf_op jit(solution)/shard_map/layer/pallas_call | solution.py:946
  164.2 5.6 %hand_over.1 = (f32[768,768]{1,0:T(8,128)}, f32[768,768]{1,0:T(8,128)}, f32[2,768]{1,0:T(2,128)}, f32[2,768]{1,0:T(2,128)}, f32[48,768]{1,0:T(8,128)}, /*index=5...) custom-call(f32[768,768]{1,0:T(8,128)} %get-tuple-element.38.block, ...), custom_call_target="tpu_custom_call" | custom-call | tf_op jit(solution)/shard_map/hand_over/pallas_call | solution.py:1037
